TPU v7x, 256 devices: a whole 4x4x8 slice. The times are simulated.
256 devices in a mesh: seq: 8 (over x, core), head: 32 (over y, z).
Axes of the slice: x: 4, y: 4, z: 8, core: 2. Of those that a mesh axis runs over, the one named last changes fastest.
Arguments:
- queries: bfloat16 [32768, 4096], P(('seq', 'head')), may hold values from -4 to 4
- keys: bfloat16 [32768, 1024], P(('seq', 'head')), may hold values from -4 to 4
- values: bfloat16 [32768, 1024], P(('seq', 'head')), may hold values from -6 to 6
- modality: int32 [32768], P(('seq', 'head')), may hold values 0 or 1
- clip_lengths: int32 [128], replicated, may hold values from 1 to 512, 32768 in all
- query_gains: float32 [2, 4096], replicated, may hold values from 0.5 to 5.2
- key_gains: float32 [2, 1024], replicated, may hold values from 0.5 to 5.2
- out_grad: bfloat16 [32768, 4096], P(('seq', 'head')), may hold values from -6 to 6
Outputs:
- attended: bfloat16 [32768, 4096], P(('seq', 'head'))
- query_grad: bfloat16 [32768, 4096], P(('seq', 'head'))
- key_grad: bfloat16 [32768, 1024], P(('seq', 'head'))
- value_grad: bfloat16 [32768, 1024], P(('seq', 'head'))
- query_gain_grad: float32 [2, 4096], replicated
- key_gain_grad: float32 [2, 1024], replicated
Inputs may be any that keep to these rules, and one draw needn't show every extreme that they name: `clip_lengths`: the clips cover the 32768 positions end to end; some clip has exactly 512 positions.
All inputs are finite; a program needn't handle non-finite values. No bound on the sum of `modality` on one device may be relied on, other than what follows from the above.
Results may differ from a plain program's by a relative error of at most 0.025.
The roundings to bfloat16 on the way count: a program that leaves them out, or rounds other values in their place, can miss the bound.
Values may be sent and summed in bfloat16 or wider, within the bound.
No kernel may reach another device: no remote copies, remote signals or barrier semaphores. Data moves between devices by JAX's collectives and lax.ppermute only.
A program may use at most 128 MiB of HBM per device.

v0:
```python
import math
import jax
import jax.numpy as jnp
from jax import lax
from jax.sharding import PartitionSpec as P

HD = 128
MOST = 512
row_block = 512


def from_behind(value, axis, steps):
    count = lax.axis_size(axis)
    first, last = (max(0, -steps), min(count, count - steps))
    return lax.ppermute(value, axis, [(source, source + steps) for source in range(first, last)])


def clip_start(clip_lengths, positions):
    order = jnp.arange(clip_lengths.shape[0], dtype=jnp.int32)
    begins = jnp.sum(jnp.where(order[None, :] < order[:, None], clip_lengths[None, :], 0), axis=1)
    chosen = jnp.where(
        begins[None, :] <= positions[:, None], begins[None, :], jnp.zeros((), jnp.int32)
    )
    return jnp.max(chosen, axis=1)


def normalize(rows, modality, gains):
    count, width = rows.shape
    shaped = rows.astype(jnp.float32).reshape(count, width // HD, HD)
    factor = lax.rsqrt(jnp.mean(shaped * shaped, axis=2, keepdims=True) + 1e-06)
    unit = shaped * factor
    gain_rows = jnp.where(modality[:, None] == 1, gains[1][None, :], gains[0][None, :]).reshape(
        count, width // HD, HD
    )
    normed = (unit * gain_rows).astype(jnp.bfloat16).reshape(count, width)
    return (normed, unit, factor, gain_rows)


def unnormalize(grad_low, unit, factor, gain_rows, modality):
    count = unit.shape[0]
    shaped = grad_low.astype(jnp.float32).reshape(unit.shape)
    along = shaped * gain_rows
    back = factor * (along - unit * jnp.mean(along * unit, axis=2, keepdims=True))
    term = (shaped * unit).reshape(count, -1)
    choose = (modality[:, None] == jnp.arange(2, dtype=jnp.int32)[None, :]).astype(jnp.float32)
    gain_part = jnp.einsum("rm,rc->mc", choose, term, precision=lax.Precision.HIGHEST)
    return (back.reshape(count, -1).astype(jnp.bfloat16), gain_part)


def spread_heads(rows, kv_heads, repeat):
    count = rows.shape[0]
    return jnp.broadcast_to(
        rows.reshape(count, kv_heads, 1, HD), (count, kv_heads, repeat, HD)
    ).reshape(count, kv_heads * repeat, HD)


def fold_heads(rows, kv_heads, repeat):
    count = rows.shape[0]
    return jnp.sum(rows.reshape(count, kv_heads, repeat, HD), axis=2)


def attend(query_norm, key_ext, value_ext, grad_rows, first, starts, block):
    rows = query_norm.shape[0]
    reach = key_ext.shape[0] - rows
    span = block + reach
    scale = 1.0 / math.sqrt(query_norm.shape[2])
    offsets = jnp.arange(span, dtype=jnp.int32)
    inside = jnp.arange(block, dtype=jnp.int32)

    def visit(carry, index):
        key_acc, value_acc = carry
        begin = index * block
        query_pos = first + begin + inside
        key_pos = first + begin - reach + offsets
        allowed = (key_pos[None, :] >= starts[:, None]) & (key_pos[None, :] <= query_pos[:, None])
        scores = (
            jnp.einsum("qnd,knd->qnk", query_norm, key_ext, preferred_element_type=jnp.float32)
            * scale
        )
        scores = jnp.where(allowed[:, None, :], scores, jnp.float32(-1e30))
        top = jnp.max(scores, axis=2, keepdims=True)
        expo = jnp.exp(scores - top)
        probs = expo / jnp.sum(expo, axis=2, keepdims=True)
        probs_low = probs.astype(jnp.bfloat16)
        attended = jnp.einsum(
            "qnk,knd->qnd", probs_low, value_ext, preferred_element_type=jnp.float32
        ).astype(jnp.bfloat16)
        delta = jnp.sum(
            grad_rows.astype(jnp.float32) * attended.astype(jnp.float32), axis=2, keepdims=True
        )
        prob_grad = jnp.einsum(
            "qnd,knd->qnk", grad_rows, value_ext, preferred_element_type=jnp.float32
        )
        score_grad = (probs * (prob_grad - delta) * scale).astype(jnp.bfloat16)
        query_grad = jnp.einsum(
            "qnk,knd->qnd", score_grad, key_ext, preferred_element_type=jnp.float32
        ).astype(jnp.bfloat16)
        key_step = jnp.einsum(
            "qnk,qnd->knd", score_grad, query_norm, preferred_element_type=jnp.float32
        )
        value_step = jnp.einsum(
            "qnk,qnd->knd", probs_low, grad_rows, preferred_element_type=jnp.float32
        )
        key_acc = key_acc + key_step
        value_acc = value_acc + value_step
        return ((key_acc, value_acc), (attended, query_grad))

    zeros = jnp.zeros(key_ext.shape, jnp.float32)
    (key_acc, value_acc), (attended, query_grad) = lax.scan(
        visit, (zeros, zeros), jnp.arange(rows // block, dtype=jnp.int32)
    )
    heads, depth = (query_norm.shape[1], query_norm.shape[2])
    return (
        attended.reshape(rows, heads, depth),
        query_grad.reshape(rows, heads, depth),
        key_acc,
        value_acc,
    )


def on_device(queries, keys, values, modality, clip_lengths, query_gains, key_gains, out_grad):
    count, width = queries.shape
    heads = width // HD
    kv_heads = keys.shape[1] // HD
    repeat = heads // kv_heads
    query_norm, query_unit, query_factor, query_gain_rows = normalize(
        queries, modality, query_gains
    )
    key_norm, key_unit, key_factor, key_gain_rows = normalize(keys, modality, key_gains)
    first = lax.axis_index(("seq", "head")) * count
    depth = (MOST + count - 1) // count
    far_keys = []
    far_values = []
    for step in range(depth, 0, -1):
        moved_key, moved_value = from_behind((key_norm, values), ("seq", "head"), step)
        far_keys.append(moved_key)
        far_values.append(moved_value)
    key_ext = jnp.concatenate(far_keys + [key_norm], 0)
    value_ext = jnp.concatenate(far_values + [values], 0)
    starts = clip_start(clip_lengths, first + jnp.arange(count, dtype=jnp.int32))
    attended, query_low, key_acc, value_acc = attend(
        query_norm.reshape(count, heads, HD),
        spread_heads(key_ext, kv_heads, repeat),
        spread_heads(value_ext, kv_heads, repeat),
        out_grad.reshape(count, heads, HD),
        first,
        starts,
        min(row_block, count),
    )
    key_acc = fold_heads(key_acc, kv_heads, repeat)
    value_acc = fold_heads(value_acc, kv_heads, repeat)
    front_key = key_acc[:MOST]
    front_value = value_acc[:MOST]
    key_total = key_acc[MOST:]
    value_total = value_acc[MOST:]
    for step in range(depth, 0, -1):
        begin = (depth - step) * count
        back_key, back_value = (
            from_behind(
                front_key[begin : begin + count].astype(jnp.bfloat16), ("seq", "head"), -step
            ).astype(jnp.float32),
            from_behind(
                front_value[begin : begin + count].astype(jnp.bfloat16), ("seq", "head"), -step
            ).astype(jnp.float32),
        )
        key_total = key_total + back_key
        value_total = value_total + back_value
    attended = attended.reshape(count, width)
    query_low = query_low.reshape(count, width)
    key_low = key_total.reshape(count, kv_heads * HD).astype(jnp.bfloat16)
    value_grad = value_total.reshape(count, kv_heads * HD).astype(jnp.bfloat16)
    query_grad, query_gain = unnormalize(
        query_low, query_unit, query_factor, query_gain_rows, modality
    )
    key_grad, key_gain = unnormalize(key_low, key_unit, key_factor, key_gain_rows, modality)
    query_gain_grad, key_gain_grad = lax.psum((query_gain, key_gain), ("seq", "head"))
    return (attended, query_grad, key_grad, value_grad, query_gain_grad, key_gain_grad)


def solution(mesh):
    return jax.shard_map(
        on_device,
        mesh=mesh,
        in_specs=(
            P(("seq", "head"), None),
            P(("seq", "head"), None),
            P(("seq", "head"), None),
            P(("seq", "head")),
            P(),
            P(),
            P(),
            P(("seq", "head"), None),
        ),
        out_specs=(
            P(("seq", "head"), None),
            P(("seq", "head"), None),
            P(("seq", "head"), None),
            P(("seq", "head"), None),
            P(),
            P(),
        ),
        check_vma=False,
    )
```

profile of v0, /device:TPU:1, one launch (start us, length us, event | category | flops | bytes accessed | tf_op | source)
XLA Modules:
  0.0 338.0 jit_solution(9499922176696073550)
XLA Ops:
  0.7 5.9 %collective-permute-start.2 = (bf16[128,1024]{1,0:T(8,128)(2,1)}, bf16[128,1024]{1,0:T(8,128)(2,1)}, u32[]{:S(2)}, u32[]{:S(2)}) collective-permute-start(bf16[128,1024]{1,0:T(8,128)(2,1)} %param.10), channel_id=1, source_target_pairs={{0,2},{1,3},{2,4},{3,5},{4,6},{5,7},{6,8},{7,9},{8,10},{9,11},{10,... | collective-permute-start | bytes 786440 | tf_op jit(solution)/shard_map/ppermute | solution.py:15
  6.5 6.6 %collective-permute-start.1 = (bf16[128,1024]{1,0:T(8,128)(2,1)}, bf16[128,1024]{1,0:T(8,128)(2,1)}, u32[]{:S(2)}, u32[]{:S(2)}) collective-permute-start(bf16[128,1024]{1,0:T(8,128)(2,1)} %param.10), channel_id=1, source_target_pairs={{0,3},{1,4},{2,5},{3,6},{4,7},{5,8},{6,9},{7,10},{8,11},{9,12},{10... | collective-permute-start | bytes 786440 | tf_op jit(solution)/shard_map/ppermute | solution.py:15
  13.1 0.7 broadcast_compare_fusion
  13.8 0.8 fusion.38
  14.6 1.1 copy.65
  16.1 3.1 collective-permute-start.6
  19.2 2.7 collective-permute-start.5
  21.9 7.0 %collective-permute-start.4 = (bf16[128,1024]{1,0:T(8,128)(2,1)S(1)}, bf16[128,1024]{1,0:T(8,128)(2,1)}, u32[]{:S(2)}, u32[]{:S(2)}) collective-permute-start(bf16[128,1024]{1,0:T(8,128)(2,1)S(1)} %multiply_convert_fusion.1), channel_id=1, source_target_pairs={{0,4},{1,5},{2,6},{3,7},{4,8},{5,9},{6,10},{7,11},{8,12},{9,13},{1... | collective-permute-start | bytes 786440 | tf_op jit(solution)/shard_map/ppermute | solution.py:15
  29.2 1.5 copy.68
  31.0 0.8 multiply_reduce_fusion.1
  31.8 2.3 copy.73
  34.1 0.7 add_rsqrt_fusion
  34.8 42.1 %collective-permute-done.4 = bf16[128,1024]{1,0:T(8,128)(2,1)} collective-permute-done((bf16[128,1024]{1,0:T(8,128)(2,1)S(1)}, bf16[128,1024]{1,0:T(8,128)(2,1)}, u32[]{:S(2)}, u32[]{:S(2)}) %collective-permute-start.4) | collective-permute-done | bytes 262176 | tf_op jit(solution)/shard_map/ppermute | solution.py:15
  77.0 1.9 collective-permute-start.7
  78.9 1.0 copy.92
  79.9 0.7 constant_dynamic-update-slice_fusion.9
  80.6 1.9 collective-permute-start
  82.5 1.0 copy.94
  83.5 9.7 %collective-permute-start.3 = (bf16[128,1024]{1,0:T(8,128)(2,1)S(1)}, bf16[128,1024]{1,0:T(8,128)(2,1)}, u32[]{:S(2)}, u32[]{:S(2)}) collective-permute-start(bf16[128,1024]{1,0:T(8,128)(2,1)S(1)} %copy-done.9), channel_id=1, source_target_pairs={{0,1},{1,2},{2,3},{3,4},{4,5},{5,6},{6,7},{7,8},{8,9},{9,10},{10,1... | collective-permute-start | bytes 786440 | tf_op jit(solution)/shard_map/ppermute | solution.py:15
  93.2 1.0 copy.93
  94.2 0.7 constant_dynamic-update-slice_fusion.8
  95.0 0.7 constant_dynamic-update-slice_fusion.7
  95.7 0.7 constant_dynamic-update-slice_fusion.6
  96.4 0.7 constant_dynamic-update-slice_fusion.5
  97.2 0.7 constant_dynamic-update-slice_fusion.4
  97.9 2.8 copy.67
  100.7 1.7 constant_dynamic-update-slice_fusion.3
  102.4 1.8 constant_dynamic-update-slice_fusion.2
  104.1 4.2 %collective-permute-done.3 = bf16[128,1024]{1,0:T(8,128)(2,1)} collective-permute-done((bf16[128,1024]{1,0:T(8,128)(2,1)S(1)}, bf16[128,1024]{1,0:T(8,128)(2,1)}, u32[]{:S(2)}, u32[]{:S(2)}) %collective-permute-start.3) | collective-permute-done | bytes 262176 | tf_op jit(solution)/shard_map/ppermute | solution.py:15
  108.3 1.7 constant_dynamic-update-slice_fusion.1
  110.0 0.7 constant_dynamic-update-slice_fusion
  110.7 2.6 copy_bitcast_fusion
  113.3 3.1 broadcast_in_dim.164
  116.4 9.4 %fusion.39 = (f32[128,32]{0,1:T(8,128)S(1)}, f32[128,32,640]{0,2,1:T(8,128)}) fusion(pred[128,640]{0,1:T(8,128)(4,1)S(1)} %compare_and_fusion, bf16[640,32,128]{0,2,1:T(8,128)(2,1)} %bitcast.117, f32[128,4096]{0,1:T(8,128)S(1)} %copy.68, f32[32,128]{1,0:T(8,128)S(1)} %bitcast.140, f32[32,128]{1,0:T(8,128)S(1)} %bitcast.136, ...), kind=kOutput, calls=%fused_computation.79 | convolution fusion | flops 683672192 | bytes 17973376 | tf_op jit(solution)/shard_map/while/body/eval_jaxpr/sub | solution.py:82
  125.8 5.4 %fusion.8 = bf16[128,32,640]{0,2,1:T(8,128)(2,1)S(1)} fusion(f32[128,32,640]{0,2,1:T(8,128)} %get-tuple-element.88, f32[128,32]{0,1:T(8,128)S(1)} %get-tuple-element.87), kind=kLoop, calls=%fused_computation.14 | loop fusion | flops 5242880 | bytes 15745024 | tf_op jit(solution)/shard_map/while/body/eval_jaxpr/convert_element_type | solution.py:84
  131.2 1.2 broadcast_in_dim.154
  132.4 3.1 multiply_reduce_fusion
  135.5 3.4 %bitcast_reduce_fusion = f32[640,8,128]{2,0,1:T(8,128)} fusion(bf16[128,32,640]{0,2,1:T(8,128)(2,1)S(1)} %fusion.8, bf16[128,32,128]{0,2,1:T(8,128)(2,1)S(1)} %bitcast.121), kind=kOutput, calls=%fused_computation.1 | convolution fusion | flops 673054720 | bytes 8912896 | tf_op jit(solution)/shard_map/while/body/eval_jaxpr/qnk,qnd->knd/dot_general | solution.py:101
  138.9 6.8 %fusion.3 = bf16[128,32,640]{0,2,1:T(8,128)(2,1)} fusion(f32[128,32]{0,1:T(8,128)S(1)} %get-tuple-element.89, f32[128,32,640]{0,2,1:T(8,128)} %get-tuple-element.88, f32[128,32]{0,1:T(8,128)S(1)} %get-tuple-element.87, bf16[640,32,128]{2,0,1:T(8,128)(2,1)S(1)} %bitcast.115, bf16[128,32,128]{0,2,1:T(8,128)(2,1)S(1)} %bitcast.122), kind=kOutput, calls=%fused_computation.6 | convolution fusion | flops 684195840 | bytes 22052864 | tf_op jit(solution)/shard_map/while/body/eval_jaxpr/qnd,knd->qnk/dot_general | solution.py:91
  145.7 4.0 %fusion.12 = (f32[128,32]{0,1:T(8,128)S(1)}, bf16[32,128,128]{2,1,0:T(8,128)(2,1)S(1)}) fusion(f32[128,4096]{0,1:T(8,128)S(1)} %copy.68, f32[32,128]{1,0:T(8,128)S(1)} %bitcast.141, f32[32,128]{1,0:T(8,128)S(1)} %bitcast.137, f32[128,32]{0,1:T(8,128)S(1)} %add_rsqrt_fusion, pred[128]{0:T(512)(128)(4,1)S(1)} %broadcast_compare_fusion, ...), kind=kOutput, calls=%fused_computation.21 | convolution fusion | flops 674754560 | bytes 13697152 | tf_op jit(solution)/shard_map/while/body/eval_jaxpr/qnk,knd->qnd/dot_general | solution.py:95
  149.8 4.0 %bitcast_reduce_fusion.1 = f32[640,8,128]{0,2,1:T(8,128)} fusion(bf16[128,32,640]{0,2,1:T(8,128)(2,1)S(1)} %copy-done.2, f32[128,4096]{0,1:T(8,128)S(1)} %copy.68, f32[32,128]{1,0:T(8,128)S(1)} %bitcast.142, f32[32,128]{1,0:T(8,128)S(1)} %bitcast.138, f32[128,32]{0,1:T(8,128)S(1)} %add_rsqrt_fusion, pred[128]{0:T(512)(128)(4,1)S(1)} %broadcast_compare_fusion), kind=kOutput, calls=%fused_computation.2 | convolution fusion | flops 675151872 | bytes 10010752 | tf_op jit(solution)/shard_map/while/body/eval_jaxpr/qnk,qnd->knd/dot_general | solution.py:98
  153.8 2.5 bitcast_multiply_fusion
  156.3 2.4 copy.80
  158.7 2.3 copy.79
  161.4 4.3 %collective-permute-start.8 = (bf16[128,8,128]{0,2,1:T(8,128)(2,1)S(1)}, bf16[128,8,128]{0,2,1:T(8,128)(2,1)S(1)}, u32[]{:S(2)}, u32[]{:S(2)}) collective-permute-start(bf16[128,8,128]{0,2,1:T(8,128)(2,1)S(1)} %get-tuple-element.79), channel_id=1, source_target_pairs={{4,0},{5,1},{6,2},{7,3},{8,4},{9,5},{10,6},{11,7},{12,8},{13,9},{1... | collective-permute-start | bytes 786440 | tf_op jit(solution)/shard_map/ppermute | solution.py:15
  165.8 3.6 %collective-permute-start.11 = (bf16[128,8,128]{0,2,1:T(8,128)(2,1)S(1)}, bf16[128,8,128]{0,2,1:T(8,128)(2,1)S(1)}, u32[]{:S(2)}, u32[]{:S(2)}) collective-permute-start(bf16[128,8,128]{0,2,1:T(8,128)(2,1)S(1)} %get-tuple-element.80), channel_id=1, source_target_pairs={{1,0},{2,1},{3,2},{4,3},{5,4},{6,5},{7,6},{8,7},{9,8},{10,9},{11,1... | collective-permute-start | bytes 786440 | tf_op jit(solution)/shard_map/ppermute | solution.py:15
  169.4 8.8 %collective-permute-start.10 = (bf16[128,8,128]{0,2,1:T(8,128)(2,1)S(1)}, bf16[128,8,128]{0,2,1:T(8,128)(2,1)S(1)}, u32[]{:S(2)}, u32[]{:S(2)}) collective-permute-start(bf16[128,8,128]{0,2,1:T(8,128)(2,1)S(1)} %get-tuple-element.81), channel_id=1, source_target_pairs={{2,0},{3,1},{4,2},{5,3},{6,4},{7,5},{8,6},{9,7},{10,8},{11,9},{12,... | collective-permute-start | bytes 786440 | tf_op jit(solution)/shard_map/ppermute | solution.py:15
  178.3 6.0 %collective-permute-start.9 = (bf16[128,8,128]{0,2,1:T(8,128)(2,1)S(1)}, bf16[128,8,128]{0,2,1:T(8,128)(2,1)S(1)}, u32[]{:S(2)}, u32[]{:S(2)}) collective-permute-start(bf16[128,8,128]{0,2,1:T(8,128)(2,1)S(1)} %get-tuple-element.82), channel_id=1, source_target_pairs={{3,0},{4,1},{5,2},{6,3},{7,4},{8,5},{9,6},{10,7},{11,8},{12,9},{13... | collective-permute-start | bytes 786440 | tf_op jit(solution)/shard_map/ppermute | solution.py:15
  184.5 1.0 fusion.35
  185.5 4.3 %collective-permute-start.12 = (bf16[128,8,128]{2,0,1:T(8,128)(2,1)}, bf16[128,8,128]{2,0,1:T(8,128)(2,1)S(1)}, u32[]{:S(2)}, u32[]{:S(2)}) collective-permute-start(bf16[128,8,128]{2,0,1:T(8,128)(2,1)} %get-tuple-element.75), channel_id=1, source_target_pairs={{4,0},{5,1},{6,2},{7,3},{8,4},{9,5},{10,6},{11,7},{12,8},{13,9},{1... | collective-permute-start | bytes 786440 | tf_op jit(solution)/shard_map/ppermute | solution.py:15
  189.8 1.1 fusion.28
  190.9 1.9 collective-permute-start.15
  192.9 2.5 collective-permute-start.14
  195.3 3.6 %collective-permute-done.10 = bf16[128,8,128]{0,2,1:T(8,128)(2,1)S(1)} collective-permute-done((bf16[128,8,128]{0,2,1:T(8,128)(2,1)S(1)}, bf16[128,8,128]{0,2,1:T(8,128)(2,1)S(1)}, u32[]{:S(2)}, u32[]{:S(2)}) %collective-permute-start.10) | collective-permute-done | bytes 262176 | tf_op jit(solution)/shard_map/ppermute | solution.py:15
  198.9 4.4 %collective-permute-start.13 = (bf16[128,8,128]{2,0,1:T(8,128)(2,1)}, bf16[128,8,128]{2,0,1:T(8,128)(2,1)}, u32[]{:S(2)}, u32[]{:S(2)}) collective-permute-start(bf16[128,8,128]{2,0,1:T(8,128)(2,1)} %get-tuple-element.78), channel_id=1, source_target_pairs={{3,0},{4,1},{5,2},{6,3},{7,4},{8,5},{9,6},{10,7},{11,8},{12,9},{13... | collective-permute-start | bytes 786440 | tf_op jit(solution)/shard_map/ppermute | solution.py:15
  203.3 13.8 %collective-permute-done.9 = bf16[128,8,128]{0,2,1:T(8,128)(2,1)S(1)} collective-permute-done((bf16[128,8,128]{0,2,1:T(8,128)(2,1)S(1)}, bf16[128,8,128]{0,2,1:T(8,128)(2,1)S(1)}, u32[]{:S(2)}, u32[]{:S(2)}) %collective-permute-start.9) | collective-permute-done | bytes 262176 | tf_op jit(solution)/shard_map/ppermute | solution.py:15
  217.1 1.0 convert_multiply_fusion
  218.8 0.9 copy.81
  219.7 0.4 fusion.26
  220.1 11.8 %collective-permute-done.14 = bf16[128,8,128]{2,0,1:T(8,128)(2,1)} collective-permute-done((bf16[128,8,128]{2,0,1:T(8,128)(2,1)}, bf16[128,8,128]{2,0,1:T(8,128)(2,1)}, u32[]{:S(2)}, u32[]{:S(2)}) %collective-permute-start.14) | collective-permute-done | bytes 262176 | tf_op jit(solution)/shard_map/ppermute | solution.py:15
  231.9 14.3 %collective-permute-done.13 = bf16[128,8,128]{2,0,1:T(8,128)(2,1)} collective-permute-done((bf16[128,8,128]{2,0,1:T(8,128)(2,1)}, bf16[128,8,128]{2,0,1:T(8,128)(2,1)}, u32[]{:S(2)}, u32[]{:S(2)}) %collective-permute-start.13) | collective-permute-done | bytes 262176 | tf_op jit(solution)/shard_map/ppermute | solution.py:15
  246.2 1.4 fusion.18
  247.8 0.9 copy.82
  248.6 89.4 %all-reduce = (f32[2,4096]{1,0:T(2,128)}, f32[2,1024]{1,0:T(2,128)}) all-reduce(f32[2,4096]{1,0:T(2,128)S(1)} %fusion.28, f32[2,1024]{1,0:T(2,128)S(1)} %fusion.26), channel_id=1, replica_groups=mesh['seq'=8,'head'=32] {'seq','head'}, use_global_device_ids=true, to_apply=%region_11.12 | all-reduce | flops 10240 | bytes 81920 | tf_op jit(solution)/shard_map/psum | solution.py:176
  (62 shorter events, 2.6 us)
Async XLA Ops:
  0.6 15.3 %copy-start.8 = (bf16[128,1024]{1,0:T(8,128)(2,1)S(1)}, bf16[128,1024]{1,0:T(8,128)(2,1)}, u32[]{:S(2)}) copy-start(bf16[128,1024]{1,0:T(8,128)(2,1)} %param.9) | copy-start | bytes 786436
  0.6 28.3 %copy-start.12 = (s32[128]{0:T(128)S(1)}, s32[128]{0:T(128)}, u32[]{:S(2)}) copy-start(s32[128]{0:T(128)} %param.12) | copy-start | bytes 1540
  0.7 28.5 %copy-start.10 = (f32[2,4096]{1,0:T(2,128)S(1)}, f32[2,4096]{1,0:T(2,128)}, u32[]{:S(2)}) copy-start(f32[2,4096]{1,0:T(2,128)} %param.13) | copy-start | bytes 98308
  0.7 101.7 %collective-permute-start.2 = (bf16[128,1024]{1,0:T(8,128)(2,1)}, bf16[128,1024]{1,0:T(8,128)(2,1)}, u32[]{:S(2)}, u32[]{:S(2)}) collective-permute-start(bf16[128,1024]{1,0:T(8,128)(2,1)} %param.10), channel_id=1, source_target_pairs={{0,2},{1,3},{2,4},{3,5},{4,6},{5,7},{6,8},{7,9},{8,10},{9,11},{10,... | collective-permute-start | bytes 786440 | tf_op jit(solution)/shard_map/ppermute | solution.py:15
  6.5 94.2 %collective-permute-start.1 = (bf16[128,1024]{1,0:T(8,128)(2,1)}, bf16[128,1024]{1,0:T(8,128)(2,1)}, u32[]{:S(2)}, u32[]{:S(2)}) collective-permute-start(bf16[128,1024]{1,0:T(8,128)(2,1)} %param.10), channel_id=1, source_target_pairs={{0,3},{1,4},{2,5},{3,6},{4,7},{5,8},{6,9},{7,10},{8,11},{9,12},{10... | collective-permute-start | bytes 786440 | tf_op jit(solution)/shard_map/ppermute | solution.py:15
  16.1 64.5 %collective-permute-start.6 = (bf16[128,1024]{1,0:T(8,128)(2,1)S(1)}, bf16[128,1024]{1,0:T(8,128)(2,1)}, u32[]{:S(2)}, u32[]{:S(2)}) collective-permute-start(bf16[128,1024]{1,0:T(8,128)(2,1)S(1)} %multiply_convert_fusion.1), channel_id=1, source_target_pairs={{0,2},{1,3},{2,4},{3,5},{4,6},{5,7},{6,8},{7,9},{8,10},{9,11},{10,... | collective-permute-start | bytes 786440 | tf_op jit(solution)/shard_map/ppermute | solution.py:15
  19.2 64.3 %collective-permute-start.5 = (bf16[128,1024]{1,0:T(8,128)(2,1)S(1)}, bf16[128,1024]{1,0:T(8,128)(2,1)}, u32[]{:S(2)}, u32[]{:S(2)}) collective-permute-start(bf16[128,1024]{1,0:T(8,128)(2,1)S(1)} %multiply_convert_fusion.1), channel_id=1, source_target_pairs={{0,3},{1,4},{2,5},{3,6},{4,7},{5,8},{6,9},{7,10},{8,11},{9,12},{10... | collective-permute-start | bytes 786440 | tf_op jit(solution)/shard_map/ppermute | solution.py:15
  21.9 55.0 %collective-permute-start.4 = (bf16[128,1024]{1,0:T(8,128)(2,1)S(1)}, bf16[128,1024]{1,0:T(8,128)(2,1)}, u32[]{:S(2)}, u32[]{:S(2)}) collective-permute-start(bf16[128,1024]{1,0:T(8,128)(2,1)S(1)} %multiply_convert_fusion.1), channel_id=1, source_target_pairs={{0,4},{1,5},{2,6},{3,7},{4,8},{5,9},{6,10},{7,11},{8,12},{9,13},{1... | collective-permute-start | bytes 786440 | tf_op jit(solution)/shard_map/ppermute | solution.py:15
  31.8 48.8 %copy-start.9 = (bf16[128,1024]{1,0:T(8,128)(2,1)S(1)}, bf16[128,1024]{1,0:T(8,128)(2,1)}, u32[]{:S(2)}) copy-start(bf16[128,1024]{1,0:T(8,128)(2,1)} %param.10) | copy-start | bytes 786436
  77.0 18.7 %collective-permute-start.7 = (bf16[128,1024]{1,0:T(8,128)(2,1)S(1)}, bf16[128,1024]{1,0:T(8,128)(2,1)S(1)}, u32[]{:S(2)}, u32[]{:S(2)}) collective-permute-start(bf16[128,1024]{1,0:T(8,128)(2,1)S(1)} %multiply_convert_fusion.1), channel_id=1, source_target_pairs={{0,1},{1,2},{2,3},{3,4},{4,5},{5,6},{6,7},{7,8},{8,9},{9,10},{10,1... | collective-permute-start | bytes 786440 | tf_op jit(solution)/shard_map/ppermute | solution.py:15
  80.6 16.5 %collective-permute-start = (bf16[128,1024]{1,0:T(8,128)(2,1)S(1)}, bf16[128,1024]{1,0:T(8,128)(2,1)S(1)}, u32[]{:S(2)}, u32[]{:S(2)}) collective-permute-start(bf16[128,1024]{1,0:T(8,128)(2,1)S(1)} %copy-done.9), channel_id=1, source_target_pairs={{0,4},{1,5},{2,6},{3,7},{4,8},{5,9},{6,10},{7,11},{8,12},{9,13},{1... | collective-permute-start | bytes 786440 | tf_op jit(solution)/shard_map/ppermute | solution.py:15
  83.5 24.7 %collective-permute-start.3 = (bf16[128,1024]{1,0:T(8,128)(2,1)S(1)}, bf16[128,1024]{1,0:T(8,128)(2,1)}, u32[]{:S(2)}, u32[]{:S(2)}) collective-permute-start(bf16[128,1024]{1,0:T(8,128)(2,1)S(1)} %copy-done.9), channel_id=1, source_target_pairs={{0,1},{1,2},{2,3},{3,4},{4,5},{5,6},{6,7},{7,8},{8,9},{9,10},{10,1... | collective-permute-start | bytes 786440 | tf_op jit(solution)/shard_map/ppermute | solution.py:15
  102.3 11.0 %copy-start.3 = (bf16[640,8,128]{0,2,1:T(8,128)(2,1)S(1)}, bf16[640,8,128]{0,2,1:T(8,128)(2,1)}, u32[]{:S(2)}) copy-start(bf16[640,8,128]{0,2,1:T(8,128)(2,1)} %copy.67) | copy-start | bytes 3932164
  125.8 5.4 %copy-start.4 = (bf16[640,8,128]{2,0,1:T(8,128)(2,1)S(1)}, bf16[640,8,128]{2,0,1:T(8,128)(2,1)}, u32[]{:S(2)}) copy-start(bf16[640,8,128]{2,0,1:T(8,128)(2,1)} %copy_bitcast_fusion) | copy-start | bytes 3932164
  131.2 1.2 copy-start.5
  135.5 10.2 %slice-start = ((s8[5242880]{0:T(1024)(128)(4,1)}), s8[1048576]{0:T(1024)(128)(4,1)S(1)}, s32[]{:S(2)}) async-start(s8[5242880]{0:T(1024)(128)(4,1)} %bitcast.118), calls=%async_computation | async-start | bytes 2097152
  138.9 6.8 %slice-start.1 = ((s8[5242880]{0:T(1024)(128)(4,1)}), s8[4194304]{0:T(1024)(128)(4,1)S(1)}, s32[]{:S(2)}) async-start(s8[5242880]{0:T(1024)(128)(4,1)} %bitcast.118), calls=%async_computation.1 | async-start | bytes 8388608
  145.7 4.1 %copy-start.2 = (bf16[128,32,640]{0,2,1:T(8,128)(2,1)S(1)}, bf16[128,32,640]{0,2,1:T(8,128)(2,1)}, u32[]{:S(2)}) copy-start(bf16[128,32,640]{0,2,1:T(8,128)(2,1)} %fusion.3) | copy-start | bytes 15728644
  156.3 4.7 %copy-start = (f32[640,8,128]{0,2,1:T(8,128)S(1)}, f32[640,8,128]{0,2,1:T(8,128)}, u32[]{:S(2)}) copy-start(f32[640,8,128]{0,2,1:T(8,128)} %bitcast_reduce_fusion.1) | copy-start | bytes 7864324
  161.0 23.3 %copy-start.6 = (f32[640,8,128]{2,0,1:T(8,128)S(1)}, f32[640,8,128]{2,0,1:T(8,128)}, u32[]{:S(2)}) copy-start(f32[640,8,128]{2,0,1:T(8,128)} %bitcast_reduce_fusion) | copy-start | bytes 7864324
  161.4 29.5 %collective-permute-start.8 = (bf16[128,8,128]{0,2,1:T(8,128)(2,1)S(1)}, bf16[128,8,128]{0,2,1:T(8,128)(2,1)S(1)}, u32[]{:S(2)}, u32[]{:S(2)}) collective-permute-start(bf16[128,8,128]{0,2,1:T(8,128)(2,1)S(1)} %get-tuple-element.79), channel_id=1, source_target_pairs={{4,0},{5,1},{6,2},{7,3},{8,4},{9,5},{10,6},{11,7},{12,8},{13,9},{1... | collective-permute-start | bytes 786440 | tf_op jit(solution)/shard_map/ppermute | solution.py:15
  165.8 27.1 %collective-permute-start.11 = (bf16[128,8,128]{0,2,1:T(8,128)(2,1)S(1)}, bf16[128,8,128]{0,2,1:T(8,128)(2,1)S(1)}, u32[]{:S(2)}, u32[]{:S(2)}) collective-permute-start(bf16[128,8,128]{0,2,1:T(8,128)(2,1)S(1)} %get-tuple-element.80), channel_id=1, source_target_pairs={{1,0},{2,1},{3,2},{4,3},{5,4},{6,5},{7,6},{8,7},{9,8},{10,9},{11,1... | collective-permute-start | bytes 786440 | tf_op jit(solution)/shard_map/ppermute | solution.py:15
  169.4 29.5 %collective-permute-start.10 = (bf16[128,8,128]{0,2,1:T(8,128)(2,1)S(1)}, bf16[128,8,128]{0,2,1:T(8,128)(2,1)S(1)}, u32[]{:S(2)}, u32[]{:S(2)}) collective-permute-start(bf16[128,8,128]{0,2,1:T(8,128)(2,1)S(1)} %get-tuple-element.81), channel_id=1, source_target_pairs={{2,0},{3,1},{4,2},{5,3},{6,4},{7,5},{8,6},{9,7},{10,8},{11,9},{12,... | collective-permute-start | bytes 786440 | tf_op jit(solution)/shard_map/ppermute | solution.py:15
  178.2 11.6 %copy-start.1 = (f32[128,32,128]{0,2,1:T(8,128)S(1)}, f32[128,32,128]{0,2,1:T(8,128)}, u32[]{:S(2)}) copy-start(f32[128,32,128]{0,2,1:T(8,128)} %get-tuple-element.73) | copy-start | bytes 6291460
  178.3 11.6 %copy-start.11 = (s32[128]{0:T(128)S(1)}, s32[128]{0:T(128)}, u32[]{:S(2)}) copy-start(s32[128]{0:T(128)} %param.11) | copy-start | bytes 1540
  178.3 38.8 %collective-permute-start.9 = (bf16[128,8,128]{0,2,1:T(8,128)(2,1)S(1)}, bf16[128,8,128]{0,2,1:T(8,128)(2,1)S(1)}, u32[]{:S(2)}, u32[]{:S(2)}) collective-permute-start(bf16[128,8,128]{0,2,1:T(8,128)(2,1)S(1)} %get-tuple-element.82), channel_id=1, source_target_pairs={{3,0},{4,1},{5,2},{6,3},{7,4},{8,5},{9,6},{10,7},{11,8},{12,9},{13... | collective-permute-start | bytes 786440 | tf_op jit(solution)/shard_map/ppermute | solution.py:15
  185.5 34.6 %collective-permute-start.12 = (bf16[128,8,128]{2,0,1:T(8,128)(2,1)}, bf16[128,8,128]{2,0,1:T(8,128)(2,1)S(1)}, u32[]{:S(2)}, u32[]{:S(2)}) collective-permute-start(bf16[128,8,128]{2,0,1:T(8,128)(2,1)} %get-tuple-element.75), channel_id=1, source_target_pairs={{4,0},{5,1},{6,2},{7,3},{8,4},{9,5},{10,6},{11,7},{12,8},{13,9},{1... | collective-permute-start | bytes 786440 | tf_op jit(solution)/shard_map/ppermute | solution.py:15
  190.9 29.2 %collective-permute-start.15 = (bf16[128,8,128]{2,0,1:T(8,128)(2,1)}, bf16[128,8,128]{2,0,1:T(8,128)(2,1)}, u32[]{:S(2)}, u32[]{:S(2)}) collective-permute-start(bf16[128,8,128]{2,0,1:T(8,128)(2,1)} %get-tuple-element.76), channel_id=1, source_target_pairs={{1,0},{2,1},{3,2},{4,3},{5,4},{6,5},{7,6},{8,7},{9,8},{10,9},{11,1... | collective-permute-start | bytes 786440 | tf_op jit(solution)/shard_map/ppermute | solution.py:15
  192.9 39.0 %collective-permute-start.14 = (bf16[128,8,128]{2,0,1:T(8,128)(2,1)}, bf16[128,8,128]{2,0,1:T(8,128)(2,1)}, u32[]{:S(2)}, u32[]{:S(2)}) collective-permute-start(bf16[128,8,128]{2,0,1:T(8,128)(2,1)} %get-tuple-element.77), channel_id=1, source_target_pairs={{2,0},{3,1},{4,2},{5,3},{6,4},{7,5},{8,6},{9,7},{10,8},{11,9},{12,... | collective-permute-start | bytes 786440 | tf_op jit(solution)/shard_map/ppermute | solution.py:15
  198.9 47.2 %collective-permute-start.13 = (bf16[128,8,128]{2,0,1:T(8,128)(2,1)}, bf16[128,8,128]{2,0,1:T(8,128)(2,1)}, u32[]{:S(2)}, u32[]{:S(2)}) collective-permute-start(bf16[128,8,128]{2,0,1:T(8,128)(2,1)} %get-tuple-element.78), channel_id=1, source_target_pairs={{3,0},{4,1},{5,2},{6,3},{7,4},{8,5},{9,6},{10,7},{11,8},{12,9},{13... | collective-permute-start | bytes 786440 | tf_op jit(solution)/shard_map/ppermute | solution.py:15
  218.1 1.6 copy-start.7
where the time goes:
time: 339 us; the launch traced here: 338 us
  waiting for transfers between devices  89.8 us (26%)
  blocking collectives  89.4 us (26%)
  starting transfers between devices  74.7 us (22%)
  local copies, waits for them, and re-layouts  36.7 us (11%)
  matrix products  32.2 us (9%)
  other arithmetic  14.2 us (4%)
    ppermute x16, waiting for transfers between devices, from_behind(): lax.ppermute(value, axis, [(source, source + steps) for source in range(f...  89.8 us
    psum x1, blocking collectives, on_device(): lax.psum((query_gain, key_gain), ('seq', 'head'))  89.4 us
    ppermute x16, starting transfers between devices, from_behind(): lax.ppermute(value, axis, [(source, source + steps) for source in range(f...  74.7 us
    unnamed x48, local copies, waits for them, and re-layouts  20.5 us
    broadcast_in_dim x4, local copies, waits for them, and re-layouts, spread_heads(): jnp.broadcast_to(rows.reshape(count, kv_heads, 1, HD), (count, kv_heads,...  9.7 us
    sub x1, matrix products, visit(): expo = jnp.exp(scores - top)  9.41 us
  transfers between devices with their start and end apart: 16, of which 6 were waited for; matrix products, arithmetic and copies ran while one was open for 8% of the time, Pallas kernels for 0%

commit v1 on v0

--- a/solution.py
+++ b/solution.py
@@ -173,7 +173,7 @@
         query_low, query_unit, query_factor, query_gain_rows, modality
     )
     key_grad, key_gain = unnormalize(key_low, key_unit, key_factor, key_gain_rows, modality)
-    query_gain_grad, key_gain_grad = lax.psum((query_gain, key_gain), ("seq", "head"))
+    query_gain_grad, key_gain_grad = lax.psum(lax.psum((query_gain, key_gain), "seq"), "head")
     return (attended, query_grad, key_grad, value_grad, query_gain_grad, key_gain_grad)
 
 

time: 339 us -> 426 us (1.26)
  the two profiles are of different devices: /device:TPU:1 before, /device:TPU:0 now
where the time goes in v1:
time: 426 us; the launch traced here: 425 us
  blocking collectives  199 us (47%)
  waiting for transfers between devices  85.1 us (20%)
  starting transfers between devices  57.3 us (13%)
  local copies, waits for them, and re-layouts  36.7 us (9%)
  matrix products  32.1 us (8%)
  other arithmetic  14.2 us (3%)
    psum x1, blocking collectives, on_device(): lax.psum(lax.psum((query_gain, key_gain), 'seq'), 'head')  143 us
    ppermute x16, waiting for transfers between devices, from_behind(): lax.ppermute(value, axis, [(source, source + steps) for source in range(f...  85.1 us
    ppermute x16, starting transfers between devices, from_behind(): lax.ppermute(value, axis, [(source, source + steps) for source in range(f...  57.3 us
    psum x1, blocking collectives, on_device(): lax.psum((query_gain, key_gain), 'seq')  55.8 us
    unnamed x48, local copies, waits for them, and re-layouts  20.6 us
    broadcast_in_dim x4, local copies, waits for them, and re-layouts, spread_heads(): jnp.broadcast_to(rows.reshape(count, kv_heads, 1, HD), (count, kv_heads,...  9.67 us
    sub x1, matrix products, visit(): expo = jnp.exp(scores - top)  9.42 us
  transfers between devices with their start and end apart: 16, of which 7 were waited for; matrix products, arithmetic and copies ran while one was open for 6% of the time, Pallas kernels for 0%

profile of v1, /device:TPU:0, one launch (start us, length us, event | category | flops | bytes accessed | tf_op | source)
XLA Modules:
  0.0 425.1 jit_solution(6167739964062252355)
XLA Ops:
  0.7 4.3 %collective-permute-start.2 = (bf16[128,1024]{1,0:T(8,128)(2,1)}, bf16[128,1024]{1,0:T(8,128)(2,1)}, u32[]{:S(2)}, u32[]{:S(2)}) collective-permute-start(bf16[128,1024]{1,0:T(8,128)(2,1)} %param.10), channel_id=1, source_target_pairs={{0,2},{1,3},{2,4},{3,5},{4,6},{5,7},{6,8},{7,9},{8,10},{9,11},{10,... | collective-permute-start | bytes 786440 | tf_op jit(solution)/shard_map/ppermute | solution.py:15
  4.9 6.9 %collective-permute-start.1 = (bf16[128,1024]{1,0:T(8,128)(2,1)}, bf16[128,1024]{1,0:T(8,128)(2,1)}, u32[]{:S(2)}, u32[]{:S(2)}) collective-permute-start(bf16[128,1024]{1,0:T(8,128)(2,1)} %param.10), channel_id=1, source_target_pairs={{0,3},{1,4},{2,5},{3,6},{4,7},{5,8},{6,9},{7,10},{8,11},{9,12},{10... | collective-permute-start | bytes 786440 | tf_op jit(solution)/shard_map/ppermute | solution.py:15
  11.8 0.7 broadcast_compare_fusion
  12.5 0.8 fusion.38
  13.2 1.1 copy.65
  14.8 4.1 collective-permute-start.6
  18.9 2.3 collective-permute-start.5
  21.2 7.3 %collective-permute-start.4 = (bf16[128,1024]{1,0:T(8,128)(2,1)S(1)}, bf16[128,1024]{1,0:T(8,128)(2,1)}, u32[]{:S(2)}, u32[]{:S(2)}) collective-permute-start(bf16[128,1024]{1,0:T(8,128)(2,1)S(1)} %multiply_convert_fusion.1), channel_id=1, source_target_pairs={{0,4},{1,5},{2,6},{3,7},{4,8},{5,9},{6,10},{7,11},{8,12},{9,13},{1... | collective-permute-start | bytes 786440 | tf_op jit(solution)/shard_map/ppermute | solution.py:15
  28.7 1.5 copy.68
  30.5 0.8 multiply_reduce_fusion.1
  31.3 2.3 copy.73
  33.6 0.7 add_rsqrt_fusion
  34.3 33.6 %collective-permute-done.4 = bf16[128,1024]{1,0:T(8,128)(2,1)} collective-permute-done((bf16[128,1024]{1,0:T(8,128)(2,1)S(1)}, bf16[128,1024]{1,0:T(8,128)(2,1)}, u32[]{:S(2)}, u32[]{:S(2)}) %collective-permute-start.4) | collective-permute-done | bytes 262176 | tf_op jit(solution)/shard_map/ppermute | solution.py:15
  67.9 1.3 collective-permute-start.7
  69.2 1.0 copy.92
  70.2 0.7 constant_dynamic-update-slice_fusion.9
  71.0 9.0 %collective-permute-start = (bf16[128,1024]{1,0:T(8,128)(2,1)S(1)}, bf16[128,1024]{1,0:T(8,128)(2,1)S(1)}, u32[]{:S(2)}, u32[]{:S(2)}) collective-permute-start(bf16[128,1024]{1,0:T(8,128)(2,1)S(1)} %copy-done.9), channel_id=1, source_target_pairs={{0,4},{1,5},{2,6},{3,7},{4,8},{5,9},{6,10},{7,11},{8,12},{9,13},{1... | collective-permute-start | bytes 786440 | tf_op jit(solution)/shard_map/ppermute | solution.py:15
  80.0 1.0 copy.94
  81.0 11.6 %collective-permute-start.3 = (bf16[128,1024]{1,0:T(8,128)(2,1)S(1)}, bf16[128,1024]{1,0:T(8,128)(2,1)}, u32[]{:S(2)}, u32[]{:S(2)}) collective-permute-start(bf16[128,1024]{1,0:T(8,128)(2,1)S(1)} %copy-done.9), channel_id=1, source_target_pairs={{0,1},{1,2},{2,3},{3,4},{4,5},{5,6},{6,7},{7,8},{8,9},{9,10},{10,1... | collective-permute-start | bytes 786440 | tf_op jit(solution)/shard_map/ppermute | solution.py:15
  92.6 1.0 copy.93
  93.6 0.7 constant_dynamic-update-slice_fusion.8
  94.4 0.7 constant_dynamic-update-slice_fusion.7
  95.1 0.7 constant_dynamic-update-slice_fusion.6
  95.8 0.7 constant_dynamic-update-slice_fusion.5
  96.5 0.7 constant_dynamic-update-slice_fusion.4
  97.3 2.8 copy.67
  100.1 1.7 constant_dynamic-update-slice_fusion.3
  101.7 1.8 constant_dynamic-update-slice_fusion.2
  103.5 1.7 constant_dynamic-update-slice_fusion.1
  105.2 0.7 constant_dynamic-update-slice_fusion
  105.9 2.6 copy_bitcast_fusion
  108.5 3.1 broadcast_in_dim.164
  111.6 9.4 %fusion.39 = (f32[128,32]{0,1:T(8,128)S(1)}, f32[128,32,640]{0,2,1:T(8,128)}) fusion(pred[128,640]{0,1:T(8,128)(4,1)S(1)} %compare_and_fusion, bf16[640,32,128]{0,2,1:T(8,128)(2,1)} %bitcast.117, f32[128,4096]{0,1:T(8,128)S(1)} %copy.68, f32[32,128]{1,0:T(8,128)S(1)} %bitcast.140, f32[32,128]{1,0:T(8,128)S(1)} %bitcast.136, ...), kind=kOutput, calls=%fused_computation.79 | convolution fusion | flops 683672192 | bytes 17973376 | tf_op jit(solution)/shard_map/while/body/eval_jaxpr/sub | solution.py:82
  121.0 5.4 %fusion.8 = bf16[128,32,640]{0,2,1:T(8,128)(2,1)S(1)} fusion(f32[128,32,640]{0,2,1:T(8,128)} %get-tuple-element.90, f32[128,32]{0,1:T(8,128)S(1)} %get-tuple-element.89), kind=kLoop, calls=%fused_computation.14 | loop fusion | flops 5242880 | bytes 15745024 | tf_op jit(solution)/shard_map/while/body/eval_jaxpr/convert_element_type | solution.py:84
  126.4 1.2 broadcast_in_dim.154
  127.6 3.1 multiply_reduce_fusion
  130.7 3.4 bitcast_reduce_fusion
  134.1 6.8 %fusion.3 = bf16[128,32,640]{0,2,1:T(8,128)(2,1)} fusion(f32[128,32]{0,1:T(8,128)S(1)} %get-tuple-element.91, f32[128,32,640]{0,2,1:T(8,128)} %get-tuple-element.90, f32[128,32]{0,1:T(8,128)S(1)} %get-tuple-element.89, bf16[640,32,128]{2,0,1:T(8,128)(2,1)S(1)} %bitcast.115, bf16[128,32,128]{0,2,1:T(8,128)(2,1)S(1)} %bitcast.122), kind=kOutput, calls=%fused_computation.6 | convolution fusion | flops 684195840 | bytes 22052864 | tf_op jit(solution)/shard_map/while/body/eval_jaxpr/qnd,knd->qnk/dot_general | solution.py:91
  140.9 4.0 fusion.12
  145.0 4.0 bitcast_reduce_fusion.1
  148.9 2.5 bitcast_multiply_fusion
  151.5 2.4 copy.80
  153.9 2.3 copy.79
  156.6 1.4 collective-permute-start.8
  158.0 1.3 collective-permute-start.11
  159.3 1.3 collective-permute-start.10
  160.6 1.4 collective-permute-start.9
  162.3 1.0 fusion.35
  163.3 1.3 collective-permute-start.12
  164.6 1.1 fusion.28
  165.7 5.1 %collective-permute-done.8 = bf16[128,8,128]{0,2,1:T(8,128)(2,1)S(1)} collective-permute-done((bf16[128,8,128]{0,2,1:T(8,128)(2,1)S(1)}, bf16[128,8,128]{0,2,1:T(8,128)(2,1)S(1)}, u32[]{:S(2)}, u32[]{:S(2)}) %collective-permute-start.8) | collective-permute-done | bytes 262176 | tf_op jit(solution)/shard_map/ppermute | solution.py:15
  170.7 1.3 collective-permute-start.15
  172.0 1.3 collective-permute-start.14
  173.3 11.1 %collective-permute-done.10 = bf16[128,8,128]{0,2,1:T(8,128)(2,1)S(1)} collective-permute-done((bf16[128,8,128]{0,2,1:T(8,128)(2,1)S(1)}, bf16[128,8,128]{0,2,1:T(8,128)(2,1)S(1)}, u32[]{:S(2)}, u32[]{:S(2)}) %collective-permute-start.10) | collective-permute-done | bytes 262176 | tf_op jit(solution)/shard_map/ppermute | solution.py:15
  184.5 1.3 collective-permute-start.13
  185.8 2.4 collective-permute-done.9
  188.2 1.0 convert_multiply_fusion
  189.9 0.9 copy.81
  191.3 14.9 %collective-permute-done.14 = bf16[128,8,128]{2,0,1:T(8,128)(2,1)} collective-permute-done((bf16[128,8,128]{2,0,1:T(8,128)(2,1)}, bf16[128,8,128]{2,0,1:T(8,128)(2,1)}, u32[]{:S(2)}, u32[]{:S(2)}) %collective-permute-start.14) | collective-permute-done | bytes 262176 | tf_op jit(solution)/shard_map/ppermute | solution.py:15
  206.2 17.9 %collective-permute-done.13 = bf16[128,8,128]{2,0,1:T(8,128)(2,1)} collective-permute-done((bf16[128,8,128]{2,0,1:T(8,128)(2,1)}, bf16[128,8,128]{2,0,1:T(8,128)(2,1)}, u32[]{:S(2)}, u32[]{:S(2)}) %collective-permute-start.13) | collective-permute-done | bytes 262176 | tf_op jit(solution)/shard_map/ppermute | solution.py:15
  224.1 1.4 fusion.18
  225.7 0.9 copy.82
  226.5 55.8 %all-reduce.1 = (f32[2,4096]{1,0:T(2,128)S(1)}, f32[2,1024]{1,0:T(2,128)S(1)}) all-reduce(f32[2,4096]{1,0:T(2,128)S(1)} %fusion.28, f32[2,1024]{1,0:T(2,128)S(1)} %fusion.26), channel_id=1, replica_groups=mesh['seq'=8,'head'=32] {'seq'}, use_global_device_ids=true, to_apply=%region_11.12 | all-reduce | flops 10240 | bytes 81920 | tf_op jit(solution)/shard_map/psum | solution.py:176
  282.3 142.7 %all-reduce = (f32[2,4096]{1,0:T(2,128)}, f32[2,1024]{1,0:T(2,128)}) all-reduce(f32[2,4096]{1,0:T(2,128)S(1)} %get-tuple-element.71, f32[2,1024]{1,0:T(2,128)S(1)} %get-tuple-element.72), channel_id=1, replica_groups=mesh['seq'=8,'head'=32] {'head'}, use_global_device_ids=true, to_apply=%region_12.13 | all-reduce | flops 10240 | bytes 81920 | tf_op jit(solution)/shard_map/psum | solution.py:176
  (63 shorter events, 3.2 us)
Async XLA Ops:
  0.6 14.0 %copy-start.8 = (bf16[128,1024]{1,0:T(8,128)(2,1)S(1)}, bf16[128,1024]{1,0:T(8,128)(2,1)}, u32[]{:S(2)}) copy-start(bf16[128,1024]{1,0:T(8,128)(2,1)} %param.9) | copy-start | bytes 786436
  0.6 27.8 %copy-start.12 = (s32[128]{0:T(128)S(1)}, s32[128]{0:T(128)}, u32[]{:S(2)}) copy-start(s32[128]{0:T(128)} %param.12) | copy-start | bytes 1540
  0.7 28.0 %copy-start.10 = (f32[2,4096]{1,0:T(2,128)S(1)}, f32[2,4096]{1,0:T(2,128)}, u32[]{:S(2)}) copy-start(f32[2,4096]{1,0:T(2,128)} %param.13) | copy-start | bytes 98308
  0.7 101.1 %collective-permute-start.2 = (bf16[128,1024]{1,0:T(8,128)(2,1)}, bf16[128,1024]{1,0:T(8,128)(2,1)}, u32[]{:S(2)}, u32[]{:S(2)}) collective-permute-start(bf16[128,1024]{1,0:T(8,128)(2,1)} %param.10), channel_id=1, source_target_pairs={{0,2},{1,3},{2,4},{3,5},{4,6},{5,7},{6,8},{7,9},{8,10},{9,11},{10,... | collective-permute-start | bytes 786440 | tf_op jit(solution)/shard_map/ppermute | solution.py:15
  4.9 95.1 %collective-permute-start.1 = (bf16[128,1024]{1,0:T(8,128)(2,1)}, bf16[128,1024]{1,0:T(8,128)(2,1)}, u32[]{:S(2)}, u32[]{:S(2)}) collective-permute-start(bf16[128,1024]{1,0:T(8,128)(2,1)} %param.10), channel_id=1, source_target_pairs={{0,3},{1,4},{2,5},{3,6},{4,7},{5,8},{6,9},{7,10},{8,11},{9,12},{10... | collective-permute-start | bytes 786440 | tf_op jit(solution)/shard_map/ppermute | solution.py:15
  14.8 56.2 %collective-permute-start.6 = (bf16[128,1024]{1,0:T(8,128)(2,1)S(1)}, bf16[128,1024]{1,0:T(8,128)(2,1)}, u32[]{:S(2)}, u32[]{:S(2)}) collective-permute-start(bf16[128,1024]{1,0:T(8,128)(2,1)S(1)} %multiply_convert_fusion.1), channel_id=1, source_target_pairs={{0,2},{1,3},{2,4},{3,5},{4,6},{5,7},{6,8},{7,9},{8,10},{9,11},{10,... | collective-permute-start | bytes 786440 | tf_op jit(solution)/shard_map/ppermute | solution.py:15
  18.9 62.2 %collective-permute-start.5 = (bf16[128,1024]{1,0:T(8,128)(2,1)S(1)}, bf16[128,1024]{1,0:T(8,128)(2,1)}, u32[]{:S(2)}, u32[]{:S(2)}) collective-permute-start(bf16[128,1024]{1,0:T(8,128)(2,1)S(1)} %multiply_convert_fusion.1), channel_id=1, source_target_pairs={{0,3},{1,4},{2,5},{3,6},{4,7},{5,8},{6,9},{7,10},{8,11},{9,12},{10... | collective-permute-start | bytes 786440 | tf_op jit(solution)/shard_map/ppermute | solution.py:15
  21.2 46.8 %collective-permute-start.4 = (bf16[128,1024]{1,0:T(8,128)(2,1)S(1)}, bf16[128,1024]{1,0:T(8,128)(2,1)}, u32[]{:S(2)}, u32[]{:S(2)}) collective-permute-start(bf16[128,1024]{1,0:T(8,128)(2,1)S(1)} %multiply_convert_fusion.1), channel_id=1, source_target_pairs={{0,4},{1,5},{2,6},{3,7},{4,8},{5,9},{6,10},{7,11},{8,12},{9,13},{1... | collective-permute-start | bytes 786440 | tf_op jit(solution)/shard_map/ppermute | solution.py:15
  31.3 39.7 %copy-start.9 = (bf16[128,1024]{1,0:T(8,128)(2,1)S(1)}, bf16[128,1024]{1,0:T(8,128)(2,1)}, u32[]{:S(2)}) copy-start(bf16[128,1024]{1,0:T(8,128)(2,1)} %param.10) | copy-start | bytes 786436
  67.9 27.1 %collective-permute-start.7 = (bf16[128,1024]{1,0:T(8,128)(2,1)S(1)}, bf16[128,1024]{1,0:T(8,128)(2,1)S(1)}, u32[]{:S(2)}, u32[]{:S(2)}) collective-permute-start(bf16[128,1024]{1,0:T(8,128)(2,1)S(1)} %multiply_convert_fusion.1), channel_id=1, source_target_pairs={{0,1},{1,2},{2,3},{3,4},{4,5},{5,6},{6,7},{7,8},{8,9},{9,10},{10,1... | collective-permute-start | bytes 786440 | tf_op jit(solution)/shard_map/ppermute | solution.py:15
  71.0 25.6 %collective-permute-start = (bf16[128,1024]{1,0:T(8,128)(2,1)S(1)}, bf16[128,1024]{1,0:T(8,128)(2,1)S(1)}, u32[]{:S(2)}, u32[]{:S(2)}) collective-permute-start(bf16[128,1024]{1,0:T(8,128)(2,1)S(1)} %copy-done.9), channel_id=1, source_target_pairs={{0,4},{1,5},{2,6},{3,7},{4,8},{5,9},{6,10},{7,11},{8,12},{9,13},{1... | collective-permute-start | bytes 786440 | tf_op jit(solution)/shard_map/ppermute | solution.py:15
  81.0 22.5 %collective-permute-start.3 = (bf16[128,1024]{1,0:T(8,128)(2,1)S(1)}, bf16[128,1024]{1,0:T(8,128)(2,1)}, u32[]{:S(2)}, u32[]{:S(2)}) collective-permute-start(bf16[128,1024]{1,0:T(8,128)(2,1)S(1)} %copy-done.9), channel_id=1, source_target_pairs={{0,1},{1,2},{2,3},{3,4},{4,5},{5,6},{6,7},{7,8},{8,9},{9,10},{10,1... | collective-permute-start | bytes 786440 | tf_op jit(solution)/shard_map/ppermute | solution.py:15
  101.7 6.8 %copy-start.3 = (bf16[640,8,128]{0,2,1:T(8,128)(2,1)S(1)}, bf16[640,8,128]{0,2,1:T(8,128)(2,1)}, u32[]{:S(2)}) copy-start(bf16[640,8,128]{0,2,1:T(8,128)(2,1)} %copy.67) | copy-start | bytes 3932164
  121.0 5.4 %copy-start.4 = (bf16[640,8,128]{2,0,1:T(8,128)(2,1)S(1)}, bf16[640,8,128]{2,0,1:T(8,128)(2,1)}, u32[]{:S(2)}) copy-start(bf16[640,8,128]{2,0,1:T(8,128)(2,1)} %copy_bitcast_fusion) | copy-start | bytes 3932164
  126.4 1.2 copy-start.5
  130.7 10.2 %slice-start = ((s8[5242880]{0:T(1024)(128)(4,1)}), s8[1048576]{0:T(1024)(128)(4,1)S(1)}, s32[]{:S(2)}) async-start(s8[5242880]{0:T(1024)(128)(4,1)} %bitcast.118), calls=%async_computation | async-start | bytes 2097152
  134.1 6.8 %slice-start.1 = ((s8[5242880]{0:T(1024)(128)(4,1)}), s8[4194304]{0:T(1024)(128)(4,1)S(1)}, s32[]{:S(2)}) async-start(s8[5242880]{0:T(1024)(128)(4,1)} %bitcast.118), calls=%async_computation.1 | async-start | bytes 8388608
  140.9 4.1 copy-start.2
  151.5 4.7 %copy-start = (f32[640,8,128]{0,2,1:T(8,128)S(1)}, f32[640,8,128]{0,2,1:T(8,128)}, u32[]{:S(2)}) copy-start(f32[640,8,128]{0,2,1:T(8,128)} %bitcast_reduce_fusion.1) | copy-start | bytes 7864324
  156.2 5.9 %copy-start.6 = (f32[640,8,128]{2,0,1:T(8,128)S(1)}, f32[640,8,128]{2,0,1:T(8,128)}, u32[]{:S(2)}) copy-start(f32[640,8,128]{2,0,1:T(8,128)} %bitcast_reduce_fusion) | copy-start | bytes 7864324
  156.6 14.1 %collective-permute-start.8 = (bf16[128,8,128]{0,2,1:T(8,128)(2,1)S(1)}, bf16[128,8,128]{0,2,1:T(8,128)(2,1)S(1)}, u32[]{:S(2)}, u32[]{:S(2)}) collective-permute-start(bf16[128,8,128]{0,2,1:T(8,128)(2,1)S(1)} %get-tuple-element.81), channel_id=1, source_target_pairs={{4,0},{5,1},{6,2},{7,3},{8,4},{9,5},{10,6},{11,7},{12,8},{13,9},{1... | collective-permute-start | bytes 786440 | tf_op jit(solution)/shard_map/ppermute | solution.py:15
  158.0 14.0 %collective-permute-start.11 = (bf16[128,8,128]{0,2,1:T(8,128)(2,1)S(1)}, bf16[128,8,128]{0,2,1:T(8,128)(2,1)S(1)}, u32[]{:S(2)}, u32[]{:S(2)}) collective-permute-start(bf16[128,8,128]{0,2,1:T(8,128)(2,1)S(1)} %get-tuple-element.82), channel_id=1, source_target_pairs={{1,0},{2,1},{3,2},{4,3},{5,4},{6,5},{7,6},{8,7},{9,8},{10,9},{11,1... | collective-permute-start | bytes 786440 | tf_op jit(solution)/shard_map/ppermute | solution.py:15
  159.3 25.1 %collective-permute-start.10 = (bf16[128,8,128]{0,2,1:T(8,128)(2,1)S(1)}, bf16[128,8,128]{0,2,1:T(8,128)(2,1)S(1)}, u32[]{:S(2)}, u32[]{:S(2)}) collective-permute-start(bf16[128,8,128]{0,2,1:T(8,128)(2,1)S(1)} %get-tuple-element.83), channel_id=1, source_target_pairs={{2,0},{3,1},{4,2},{5,3},{6,4},{7,5},{8,6},{9,7},{10,8},{11,9},{12,... | collective-permute-start | bytes 786440 | tf_op jit(solution)/shard_map/ppermute | solution.py:15
  160.6 3.9 copy-start.1
  160.6 3.9 copy-start.11
  160.6 27.5 %collective-permute-start.9 = (bf16[128,8,128]{0,2,1:T(8,128)(2,1)S(1)}, bf16[128,8,128]{0,2,1:T(8,128)(2,1)S(1)}, u32[]{:S(2)}, u32[]{:S(2)}) collective-permute-start(bf16[128,8,128]{0,2,1:T(8,128)(2,1)S(1)} %get-tuple-element.84), channel_id=1, source_target_pairs={{3,0},{4,1},{5,2},{6,3},{7,4},{8,5},{9,6},{10,7},{11,8},{12,9},{13... | collective-permute-start | bytes 786440 | tf_op jit(solution)/shard_map/ppermute | solution.py:15
  163.3 27.9 %collective-permute-start.12 = (bf16[128,8,128]{2,0,1:T(8,128)(2,1)}, bf16[128,8,128]{2,0,1:T(8,128)(2,1)S(1)}, u32[]{:S(2)}, u32[]{:S(2)}) collective-permute-start(bf16[128,8,128]{2,0,1:T(8,128)(2,1)} %get-tuple-element.77), channel_id=1, source_target_pairs={{4,0},{5,1},{6,2},{7,3},{8,4},{9,5},{10,6},{11,7},{12,8},{13,9},{1... | collective-permute-start | bytes 786440 | tf_op jit(solution)/shard_map/ppermute | solution.py:15
  170.7 20.6 %collective-permute-start.15 = (bf16[128,8,128]{2,0,1:T(8,128)(2,1)}, bf16[128,8,128]{2,0,1:T(8,128)(2,1)}, u32[]{:S(2)}, u32[]{:S(2)}) collective-permute-start(bf16[128,8,128]{2,0,1:T(8,128)(2,1)} %get-tuple-element.78), channel_id=1, source_target_pairs={{1,0},{2,1},{3,2},{4,3},{5,4},{6,5},{7,6},{8,7},{9,8},{10,9},{11,1... | collective-permute-start | bytes 786440 | tf_op jit(solution)/shard_map/ppermute | solution.py:15
  172.0 34.2 %collective-permute-start.14 = (bf16[128,8,128]{2,0,1:T(8,128)(2,1)}, bf16[128,8,128]{2,0,1:T(8,128)(2,1)}, u32[]{:S(2)}, u32[]{:S(2)}) collective-permute-start(bf16[128,8,128]{2,0,1:T(8,128)(2,1)} %get-tuple-element.79), channel_id=1, source_target_pairs={{2,0},{3,1},{4,2},{5,3},{6,4},{7,5},{8,6},{9,7},{10,8},{11,9},{12,... | collective-permute-start | bytes 786440 | tf_op jit(solution)/shard_map/ppermute | solution.py:15
  184.5 39.6 %collective-permute-start.13 = (bf16[128,8,128]{2,0,1:T(8,128)(2,1)}, bf16[128,8,128]{2,0,1:T(8,128)(2,1)}, u32[]{:S(2)}, u32[]{:S(2)}) collective-permute-start(bf16[128,8,128]{2,0,1:T(8,128)(2,1)} %get-tuple-element.80), channel_id=1, source_target_pairs={{3,0},{4,1},{5,2},{6,3},{7,4},{8,5},{9,6},{10,7},{11,8},{12,9},{13... | collective-permute-start | bytes 786440 | tf_op jit(solution)/shard_map/ppermute | solution.py:15
  189.2 1.6 copy-start.7
